TPU v7x, 512 devices: a whole 4x8x8 slice. The times are simulated.
512 devices in a mesh: tm: 8 (over z), rows: 64 (over x, y, core).
Axes of the slice: x: 4, y: 8, z: 8, core: 2. Of those that a mesh axis runs over, the one named last changes fastest.
Arguments:
- features: bfloat16 [32, 96, 128, 256], P('tm', None, 'rows'), may hold values from -6 to 6
- gain_first: float32 [96], replicated, may hold values from 0.1 to 1.9
- conv_first: bfloat16 [3, 3, 3, 96, 96], replicated, may hold values from -0.125 to 0.125
- gain_second: float32 [96], replicated, may hold values from 0.1 to 1.9
- conv_second: bfloat16 [3, 3, 3, 96, 96], replicated, may hold values from -0.125 to 0.125
Outputs:
- decoded: bfloat16 [32, 96, 128, 256], P('tm', None, 'rows')
All inputs are finite; a program needn't handle non-finite values.
Results may differ from a plain program's by a relative error of at most 0.004.
Values may be sent and summed in bfloat16 or wider, within the bound.
A program may use at most 64 MiB of HBM per device.

v0:
```python
import jax
import jax.numpy as jnp
from jax import lax
from jax.sharding import PartitionSpec as P

epsilon = 1e-06


def shifted(value, axis, by):
    peers = lax.axis_size(axis)
    pairs = [(i, i + by) for i in range(peers) if 0 <= i + by < peers]
    return lax.ppermute(value, axis, pairs)


def padded(cells, sides, width):
    for axis, dim in sides:
        count = lax.axis_size(axis)
        ends = count - 1
        head = lax.slice_in_dim(cells, 0, width, axis=dim)
        tail = lax.slice_in_dim(cells, cells.shape[dim] - width, cells.shape[dim], axis=dim)
        cells = jnp.concatenate(
            [
                lax.ppermute(tail, axis, [(i, (i + 1) % count) for i in range(ends)]),
                cells,
                lax.ppermute(head, axis, [((i + 1) % count, i) for i in range(ends)]),
            ],
            axis=dim,
        )
    return cells


def channel_norm(values, gain):
    mean_square = jnp.mean(values * values, axis=1, keepdims=True)
    return values * lax.rsqrt(mean_square + epsilon) * gain[None, :, None, None]


def conv_valid(extended, kernel):
    frames_out = extended.shape[0] - 2
    rows_out = extended.shape[2] - 2
    columns = extended.shape[3]
    out_chan = kernel.shape[3]
    in_chan = kernel.shape[4]

    def one_frame(position):
        slab = lax.dynamic_slice_in_dim(extended, position, 3, 0)
        summed = jnp.zeros((out_chan, rows_out, columns), jnp.float32)
        for tap_time in range(3):
            for tap_row in range(3):
                window = slab[tap_time, :, tap_row : tap_row + rows_out, :]
                stacked = kernel[tap_time, tap_row].reshape(3 * out_chan, in_chan)
                product = jnp.einsum(
                    "oc,chw->ohw", stacked, window, preferred_element_type=jnp.float32
                )
                product = product.reshape(3, out_chan, rows_out, columns)
                before = jnp.pad(product[0], ((0, 0), (0, 0), (1, 0)))[..., :columns]
                after = jnp.pad(product[2], ((0, 0), (0, 0), (0, 1)))[..., 1:]
                summed = summed + before + product[1] + after
        return summed

    return lax.map(one_frame, jnp.arange(frames_out, dtype=jnp.int32))


def on_device(features, gain_first, conv_first, gain_second, conv_second):
    frame_count = features.shape[0]
    first = jax.nn.silu(channel_norm(features.astype(jnp.float32), gain_first)).astype(jnp.bfloat16)
    earlier = shifted(first[frame_count - 2 :], "tm", 1)
    extended = jnp.concatenate([earlier, first], axis=0)
    extended = padded(extended, (("rows", 2),), 1)
    hidden = conv_valid(extended, conv_first)
    row_mask = jnp.ones((1, 1, 1, 1), jnp.float32)
    second = (jax.nn.silu(channel_norm(hidden, gain_second)) * row_mask).astype(jnp.bfloat16)
    earlier_second = shifted(second[frame_count - 2 :], "tm", 1)
    extended_second = jnp.concatenate([earlier_second, second], axis=0)
    ready = padded(extended_second, (("rows", 2),), 1)
    mixed = conv_valid(ready, conv_second)
    return (mixed + features.astype(jnp.float32)).astype(jnp.bfloat16)


def solution(mesh):
    placed = (P("tm", None, "rows", None), P(), P(), P(), P())
    return jax.shard_map(
        on_device,
        mesh=mesh,
        in_specs=placed,
        out_specs=P("tm", None, "rows", None),
        check_vma=False,
    )
```

profile of v0, /device:TPU:219, one launch (start us, length us, event | category | flops | bytes accessed | tf_op | source)
XLA Modules:
  0.0 134.0 jit_solution(10479799476374643153)
XLA Ops:
  0.0 1.1 fusion.74
  1.1 1.3 fusion.81
  2.5 5.2 %collective-permute-start = (bf16[2,96,2,256]{3,1,2,0:T(8,128)(2,1)S(1)}, bf16[2,96,2,256]{3,1,2,0:T(8,128)(2,1)S(1)}, u32[]{:S(2)}, u32[]{:S(2)}) collective-permute-start(bf16[2,96,2,256]{3,1,2,0:T(8,128)(2,1)S(1)} %slice.888), channel_id=1, source_target_pairs={{0,64},{64,128},{128,192},{192,256},{256,320},{320,384},{384,448},... | collective-permute-start | bytes 589832 | tf_op jit(solution)/shard_map/ppermute | solution.py:12
  7.7 3.5 %collective-permute-done = bf16[2,96,2,256]{3,1,2,0:T(8,128)(2,1)S(1)} collective-permute-done((bf16[2,96,2,256]{3,1,2,0:T(8,128)(2,1)S(1)}, bf16[2,96,2,256]{3,1,2,0:T(8,128)(2,1)S(1)}, u32[]{:S(2)}, u32[]{:S(2)}) %collective-permute-start) | collective-permute-done | bytes 196640 | tf_op jit(solution)/shard_map/ppermute | solution.py:12
  11.3 5.8 %collective-permute-start.1 = (bf16[6,96,1,256]{3,1,2,0:T(8,128)(2,1)S(1)}, bf16[6,96,1,256]{3,1,2,0:T(8,128)(2,1)S(1)}, u32[]{:S(2)}, u32[]{:S(2)}) collective-permute-start(bf16[6,96,1,256]{3,1,2,0:T(8,128)(2,1)S(1)} %get-tuple-element.239), channel_id=1, source_target_pairs={{0,1},{1,2},{2,3},{3,4},{4,5},{5,6},{6,7},{7,8},{8,9},{9,10},{10,1... | collective-permute-start | bytes 884744 | tf_op jit(solution)/shard_map/ppermute | solution.py:23
  17.1 1.9 %collective-permute-start.2 = (bf16[6,96,1,256]{3,1,2,0:T(8,128)(2,1)S(1)}, bf16[6,96,1,256]{3,1,2,0:T(8,128)(2,1)S(1)}, u32[]{:S(2)}, u32[]{:S(2)}) collective-permute-start(bf16[6,96,1,256]{3,1,2,0:T(8,128)(2,1)S(1)} %get-tuple-element.240), channel_id=1, source_target_pairs={{1,0},{2,1},{3,2},{4,3},{5,4},{6,5},{7,6},{8,7},{9,8},{10,9},{11,1... | collective-permute-start | bytes 884744 | tf_op jit(solution)/shard_map/ppermute | solution.py:25
  19.1 1.7 %collective-permute-done.1 = bf16[6,96,1,256]{3,1,2,0:T(8,128)(2,1)S(1)} collective-permute-done((bf16[6,96,1,256]{3,1,2,0:T(8,128)(2,1)S(1)}, bf16[6,96,1,256]{3,1,2,0:T(8,128)(2,1)S(1)}, u32[]{:S(2)}, u32[]{:S(2)}) %collective-permute-start.1) | collective-permute-done | bytes 294944 | tf_op jit(solution)/shard_map/ppermute | solution.py:23
  20.8 5.6 %collective-permute-done.2 = bf16[6,96,1,256]{3,1,2,0:T(8,128)(2,1)S(1)} collective-permute-done((bf16[6,96,1,256]{3,1,2,0:T(8,128)(2,1)S(1)}, bf16[6,96,1,256]{3,1,2,0:T(8,128)(2,1)S(1)}, u32[]{:S(2)}, u32[]{:S(2)}) %collective-permute-start.2) | collective-permute-done | bytes 294944 | tf_op jit(solution)/shard_map/ppermute | solution.py:25
  26.6 1.0 broadcast.108.clone
  27.5 39.8 %while.24 = (s32[]{:T(128)}, f32[4,96,2,256]{3,1,2,0:T(8,128)}, s32[4]{0:T(128)S(1)}, bf16[6,96,4,256]{3,1,2,0:T(8,128)(2,1)S(1)}, bf16[3,3,3,96,96]{4,3,2,1,0:T...) while((s32[]{:T(128)}, f32[4,96,2,256]{3,1,2,0:T(8,128)}, s32[4]{0:T(128)S(1)}, ...), condition=%wide.region_2.3_spmd, body=%wide.region_1.2_spmd.sunk | while | flops 256081920 | bytes 20638492 | solution.py:60
  27.5 0.6 dynamic_slice.27
  30.1 1.9 %fusion.164 = (bf16[1,1,3,96,96]{4,3,2,1,0:T(8,128)(2,1)S(1)}, bf16[1,1,3,96,96]{4,3,2,1,0:T(8,128)(2,1)S(1)}, bf16[1,1,3,96,96]{4,3,2,1,0:T(8,128)(2,1)S(1)}, b...) fusion(bf16[3,3,3,96,96]{4,3,2,1,0:T(8,128)(2,1)} %get-tuple-el, ...), kind=kLoop, calls=%fused_computation.172.clone.1 | loop fusion | bytes 995328 | tf_op jit(solution)/shard_map/while/body/eval_jaxpr/slice | solution.py:50
  32.7 1.1 convolution_bitcast_fusion.37
  33.9 0.2 convolution_bitcast_fusion.41
  34.1 0.6 copy-done
  35.7 1.7 %fusion.170 = f32[4,96,2,256]{3,1,2,0:T(8,128)} fusion(f32[4,96,2,256]{3,1,2,0:T(8,128)} %get-tuple-element.422, s32[]{:T(128)} %get-tuple-element.421, f32[96,2,256]{2,0,1:T(8,128)S(1)} %get-tuple-element.353, f32[96,2,256]{2,0,1:T(8,128)S(1)} %get-tuple-element.354, f32[288,2,256]{2,0,1:T(8,128)S(1)} %convolution_bitcast_fusion.36, ...), kind=kLoop, calls=%fused_computation.54.clone.1 | loop fusion | flops 1277952 | bytes 5505536 | tf_op jit(solution)/shard_map/while/body/jit(dynamic_update_index_in_dim)/dynamic_update_slice | solution.py:60
  37.5 0.6 dynamic_slice.27
  40.0 1.9 %fusion.164 = (bf16[1,1,3,96,96]{4,3,2,1,0:T(8,128)(2,1)S(1)}, bf16[1,1,3,96,96]{4,3,2,1,0:T(8,128)(2,1)S(1)}, bf16[1,1,3,96,96]{4,3,2,1,0:T(8,128)(2,1)S(1)}, b...) fusion(bf16[3,3,3,96,96]{4,3,2,1,0:T(8,128)(2,1)} %get-tuple-el, ...), kind=kLoop, calls=%fused_computation.172.clone.1 | loop fusion | bytes 995328 | tf_op jit(solution)/shard_map/while/body/eval_jaxpr/slice | solution.py:50
  42.6 1.1 convolution_bitcast_fusion.37
  43.8 0.2 convolution_bitcast_fusion.41
  44.0 0.6 copy-done
  45.7 1.7 %fusion.170 = f32[4,96,2,256]{3,1,2,0:T(8,128)} fusion(f32[4,96,2,256]{3,1,2,0:T(8,128)} %get-tuple-element.422, s32[]{:T(128)} %get-tuple-element.421, f32[96,2,256]{2,0,1:T(8,128)S(1)} %get-tuple-element.353, f32[96,2,256]{2,0,1:T(8,128)S(1)} %get-tuple-element.354, f32[288,2,256]{2,0,1:T(8,128)S(1)} %convolution_bitcast_fusion.36, ...), kind=kLoop, calls=%fused_computation.54.clone.1 | loop fusion | flops 1277952 | bytes 5505536 | tf_op jit(solution)/shard_map/while/body/jit(dynamic_update_index_in_dim)/dynamic_update_slice | solution.py:60
  47.4 0.6 dynamic_slice.27
  49.9 1.9 %fusion.164 = (bf16[1,1,3,96,96]{4,3,2,1,0:T(8,128)(2,1)S(1)}, bf16[1,1,3,96,96]{4,3,2,1,0:T(8,128)(2,1)S(1)}, bf16[1,1,3,96,96]{4,3,2,1,0:T(8,128)(2,1)S(1)}, b...) fusion(bf16[3,3,3,96,96]{4,3,2,1,0:T(8,128)(2,1)} %get-tuple-el, ...), kind=kLoop, calls=%fused_computation.172.clone.1 | loop fusion | bytes 995328 | tf_op jit(solution)/shard_map/while/body/eval_jaxpr/slice | solution.py:50
  52.6 1.1 convolution_bitcast_fusion.37
  54.0 0.6 copy-done
  55.6 1.7 %fusion.170 = f32[4,96,2,256]{3,1,2,0:T(8,128)} fusion(f32[4,96,2,256]{3,1,2,0:T(8,128)} %get-tuple-element.422, s32[]{:T(128)} %get-tuple-element.421, f32[96,2,256]{2,0,1:T(8,128)S(1)} %get-tuple-element.353, f32[96,2,256]{2,0,1:T(8,128)S(1)} %get-tuple-element.354, f32[288,2,256]{2,0,1:T(8,128)S(1)} %convolution_bitcast_fusion.36, ...), kind=kLoop, calls=%fused_computation.54.clone.1 | loop fusion | flops 1277952 | bytes 5505536 | tf_op jit(solution)/shard_map/while/body/jit(dynamic_update_index_in_dim)/dynamic_update_slice | solution.py:60
  57.4 0.6 dynamic_slice.27
  59.9 1.9 %fusion.164 = (bf16[1,1,3,96,96]{4,3,2,1,0:T(8,128)(2,1)S(1)}, bf16[1,1,3,96,96]{4,3,2,1,0:T(8,128)(2,1)S(1)}, bf16[1,1,3,96,96]{4,3,2,1,0:T(8,128)(2,1)S(1)}, b...) fusion(bf16[3,3,3,96,96]{4,3,2,1,0:T(8,128)(2,1)} %get-tuple-el, ...), kind=kLoop, calls=%fused_computation.172.clone.1 | loop fusion | bytes 995328 | tf_op jit(solution)/shard_map/while/body/eval_jaxpr/slice | solution.py:50
  62.5 1.1 convolution_bitcast_fusion.37
  63.9 0.6 copy-done
  65.5 1.7 %fusion.170 = f32[4,96,2,256]{3,1,2,0:T(8,128)} fusion(f32[4,96,2,256]{3,1,2,0:T(8,128)} %get-tuple-element.422, s32[]{:T(128)} %get-tuple-element.421, f32[96,2,256]{2,0,1:T(8,128)S(1)} %get-tuple-element.353, f32[96,2,256]{2,0,1:T(8,128)S(1)} %get-tuple-element.354, f32[288,2,256]{2,0,1:T(8,128)S(1)} %convolution_bitcast_fusion.36, ...), kind=kLoop, calls=%fused_computation.54.clone.1 | loop fusion | flops 1277952 | bytes 5505536 | tf_op jit(solution)/shard_map/while/body/jit(dynamic_update_index_in_dim)/dynamic_update_slice | solution.py:60
  67.3 1.2 multiply_reduce_fusion
  68.5 1.4 %multiply_convert_fusion = bf16[4,96,2,256]{3,1,2,0:T(8,128)(2,1)S(1)} fusion(f32[4,96,2,256]{3,1,2,0:T(8,128)} %get-tuple-element.135, f32[96]{0:T(128)S(1)} %copy-done.2, f32[4,2,256]{2,1,0:T(2,128)S(1)} %add_rsqrt_fusion), kind=kLoop, calls=%fused_computation.160 | loop fusion | flops 1376256 | bytes 1188224 | tf_op jit(solution)/shard_map/convert_element_type | solution.py:71
  70.0 5.3 %collective-permute-start.3 = (bf16[2,96,2,256]{3,1,2,0:T(8,128)(2,1)S(1)}, bf16[2,96,2,256]{3,1,2,0:T(8,128)(2,1)S(1)}, u32[]{:S(2)}, u32[]{:S(2)}) collective-permute-start(bf16[2,96,2,256]{3,1,2,0:T(8,128)(2,1)S(1)} %slice.891), channel_id=1, source_target_pairs={{0,64},{64,128},{128,192},{192,256},{256,320},{320,384},{384,448},... | collective-permute-start | bytes 589832 | tf_op jit(solution)/shard_map/ppermute | solution.py:12
  75.3 2.6 %collective-permute-done.3 = bf16[2,96,2,256]{3,1,2,0:T(8,128)(2,1)S(1)} collective-permute-done((bf16[2,96,2,256]{3,1,2,0:T(8,128)(2,1)S(1)}, bf16[2,96,2,256]{3,1,2,0:T(8,128)(2,1)S(1)}, u32[]{:S(2)}, u32[]{:S(2)}) %collective-permute-start.3) | collective-permute-done | bytes 196640 | tf_op jit(solution)/shard_map/ppermute | solution.py:12
  77.9 3.5 %collective-permute-start.4 = (bf16[6,96,1,256]{3,1,2,0:T(8,128)(2,1)S(1)}, bf16[6,96,1,256]{3,1,2,0:T(8,128)(2,1)S(1)}, u32[]{:S(2)}, u32[]{:S(2)}) collective-permute-start(bf16[6,96,1,256]{3,1,2,0:T(8,128)(2,1)S(1)} %get-tuple-element.237), channel_id=1, source_target_pairs={{0,1},{1,2},{2,3},{3,4},{4,5},{5,6},{6,7},{7,8},{8,9},{9,10},{10,1... | collective-permute-start | bytes 884744 | tf_op jit(solution)/shard_map/ppermute | solution.py:23
  81.4 1.9 %collective-permute-start.5 = (bf16[6,96,1,256]{3,1,2,0:T(8,128)(2,1)S(1)}, bf16[6,96,1,256]{3,1,2,0:T(8,128)(2,1)S(1)}, u32[]{:S(2)}, u32[]{:S(2)}) collective-permute-start(bf16[6,96,1,256]{3,1,2,0:T(8,128)(2,1)S(1)} %get-tuple-element.238), channel_id=1, source_target_pairs={{1,0},{2,1},{3,2},{4,3},{5,4},{6,5},{7,6},{8,7},{9,8},{10,9},{11,1... | collective-permute-start | bytes 884744 | tf_op jit(solution)/shard_map/ppermute | solution.py:25
  83.4 1.7 %collective-permute-done.4 = bf16[6,96,1,256]{3,1,2,0:T(8,128)(2,1)S(1)} collective-permute-done((bf16[6,96,1,256]{3,1,2,0:T(8,128)(2,1)S(1)}, bf16[6,96,1,256]{3,1,2,0:T(8,128)(2,1)S(1)}, u32[]{:S(2)}, u32[]{:S(2)}) %collective-permute-start.4) | collective-permute-done | bytes 294944 | tf_op jit(solution)/shard_map/ppermute | solution.py:23
  85.1 5.6 %collective-permute-done.5 = bf16[6,96,1,256]{3,1,2,0:T(8,128)(2,1)S(1)} collective-permute-done((bf16[6,96,1,256]{3,1,2,0:T(8,128)(2,1)S(1)}, bf16[6,96,1,256]{3,1,2,0:T(8,128)(2,1)S(1)}, u32[]{:S(2)}, u32[]{:S(2)}) %collective-permute-start.5) | collective-permute-done | bytes 294944 | tf_op jit(solution)/shard_map/ppermute | solution.py:25
  90.9 1.0 broadcast.108
  91.8 39.7 %while.25 = (s32[]{:T(128)}, f32[4,96,2,256]{3,1,2,0:T(8,128)}, s32[4]{0:T(128)S(1)}, bf16[6,96,4,256]{3,1,2,0:T(8,128)(2,1)S(1)}, bf16[3,3,3,96,96]{4,3,2,1,0:T...) while((s32[]{:T(128)}, f32[4,96,2,256]{3,1,2,0:T(8,128)}, s32[4]{0:T(128)S(1)}, ...), condition=%wide.region_5.6_spmd, body=%wide.region_4.5_spmd.sunk | while | flops 256081920 | bytes 20638492 | solution.py:60
  91.8 0.6 dynamic_slice.28
  94.3 1.9 %fusion.180 = (bf16[1,1,3,96,96]{4,3,2,1,0:T(8,128)(2,1)S(1)}, bf16[1,1,3,96,96]{4,3,2,1,0:T(8,128)(2,1)S(1)}, bf16[1,1,3,96,96]{4,3,2,1,0:T(8,128)(2,1)S(1)}, b...) fusion(bf16[3,3,3,96,96]{4,3,2,1,0:T(8,128)(2,1)} %get-tuple-el, ...), kind=kLoop, calls=%fused_computation.182.clone.1 | loop fusion | bytes 995328 | tf_op jit(solution)/shard_map/while/body/eval_jaxpr/slice | solution.py:50
  97.0 1.1 convolution_bitcast_fusion.46
  98.4 0.6 copy-done.1
  100.0 1.7 %fusion.186 = f32[4,96,2,256]{3,1,2,0:T(8,128)} fusion(f32[4,96,2,256]{3,1,2,0:T(8,128)} %get-tuple-element.452, s32[]{:T(128)} %get-tuple-element.451, f32[96,2,256]{2,0,1:T(8,128)S(1)} %get-tuple-element.385, f32[96,2,256]{2,0,1:T(8,128)S(1)} %get-tuple-element.386, f32[288,2,256]{2,0,1:T(8,128)S(1)} %convolution_bitcast_fusion.45, ...), kind=kLoop, calls=%fused_computation.127.clone.1 | loop fusion | flops 1277952 | bytes 5505536 | tf_op jit(solution)/shard_map/while/body/jit(dynamic_update_index_in_dim)/dynamic_update_slice | solution.py:60
  101.7 0.6 dynamic_slice.28
  104.3 1.9 %fusion.180 = (bf16[1,1,3,96,96]{4,3,2,1,0:T(8,128)(2,1)S(1)}, bf16[1,1,3,96,96]{4,3,2,1,0:T(8,128)(2,1)S(1)}, bf16[1,1,3,96,96]{4,3,2,1,0:T(8,128)(2,1)S(1)}, b...) fusion(bf16[3,3,3,96,96]{4,3,2,1,0:T(8,128)(2,1)} %get-tuple-el, ...), kind=kLoop, calls=%fused_computation.182.clone.1 | loop fusion | bytes 995328 | tf_op jit(solution)/shard_map/while/body/eval_jaxpr/slice | solution.py:50
  106.9 1.1 convolution_bitcast_fusion.46
  108.3 0.6 copy-done.1
  109.9 1.7 %fusion.186 = f32[4,96,2,256]{3,1,2,0:T(8,128)} fusion(f32[4,96,2,256]{3,1,2,0:T(8,128)} %get-tuple-element.452, s32[]{:T(128)} %get-tuple-element.451, f32[96,2,256]{2,0,1:T(8,128)S(1)} %get-tuple-element.385, f32[96,2,256]{2,0,1:T(8,128)S(1)} %get-tuple-element.386, f32[288,2,256]{2,0,1:T(8,128)S(1)} %convolution_bitcast_fusion.45, ...), kind=kLoop, calls=%fused_computation.127.clone.1 | loop fusion | flops 1277952 | bytes 5505536 | tf_op jit(solution)/shard_map/while/body/jit(dynamic_update_index_in_dim)/dynamic_update_slice | solution.py:60
  111.7 0.6 dynamic_slice.28
  114.2 1.9 %fusion.180 = (bf16[1,1,3,96,96]{4,3,2,1,0:T(8,128)(2,1)S(1)}, bf16[1,1,3,96,96]{4,3,2,1,0:T(8,128)(2,1)S(1)}, bf16[1,1,3,96,96]{4,3,2,1,0:T(8,128)(2,1)S(1)}, b...) fusion(bf16[3,3,3,96,96]{4,3,2,1,0:T(8,128)(2,1)} %get-tuple-el, ...), kind=kLoop, calls=%fused_computation.182.clone.1 | loop fusion | bytes 995328 | tf_op jit(solution)/shard_map/while/body/eval_jaxpr/slice | solution.py:50
  116.8 1.1 convolution_bitcast_fusion.46
  118.2 0.6 copy-done.1
  119.9 1.7 %fusion.186 = f32[4,96,2,256]{3,1,2,0:T(8,128)} fusion(f32[4,96,2,256]{3,1,2,0:T(8,128)} %get-tuple-element.452, s32[]{:T(128)} %get-tuple-element.451, f32[96,2,256]{2,0,1:T(8,128)S(1)} %get-tuple-element.385, f32[96,2,256]{2,0,1:T(8,128)S(1)} %get-tuple-element.386, f32[288,2,256]{2,0,1:T(8,128)S(1)} %convolution_bitcast_fusion.45, ...), kind=kLoop, calls=%fused_computation.127.clone.1 | loop fusion | flops 1277952 | bytes 5505536 | tf_op jit(solution)/shard_map/while/body/jit(dynamic_update_index_in_dim)/dynamic_update_slice | solution.py:60
  121.6 0.6 dynamic_slice.28
  124.1 1.9 %fusion.180 = (bf16[1,1,3,96,96]{4,3,2,1,0:T(8,128)(2,1)S(1)}, bf16[1,1,3,96,96]{4,3,2,1,0:T(8,128)(2,1)S(1)}, bf16[1,1,3,96,96]{4,3,2,1,0:T(8,128)(2,1)S(1)}, b...) fusion(bf16[3,3,3,96,96]{4,3,2,1,0:T(8,128)(2,1)} %get-tuple-el, ...), kind=kLoop, calls=%fused_computation.182.clone.1 | loop fusion | bytes 995328 | tf_op jit(solution)/shard_map/while/body/eval_jaxpr/slice | solution.py:50
  126.8 1.1 convolution_bitcast_fusion.46
  128.2 0.6 copy-done.1
  129.8 1.7 %fusion.186 = f32[4,96,2,256]{3,1,2,0:T(8,128)} fusion(f32[4,96,2,256]{3,1,2,0:T(8,128)} %get-tuple-element.452, s32[]{:T(128)} %get-tuple-element.451, f32[96,2,256]{2,0,1:T(8,128)S(1)} %get-tuple-element.385, f32[96,2,256]{2,0,1:T(8,128)S(1)} %get-tuple-element.386, f32[288,2,256]{2,0,1:T(8,128)S(1)} %convolution_bitcast_fusion.45, ...), kind=kLoop, calls=%fused_computation.127.clone.1 | loop fusion | flops 1277952 | bytes 5505536 | tf_op jit(solution)/shard_map/while/body/jit(dynamic_update_index_in_dim)/dynamic_update_slice | solution.py:60
  131.6 1.3 fusion.82
  132.9 1.2 copy.11
  (122 shorter events, 15.9 us)
Async XLA Ops:
  2.5 8.8 %collective-permute-start = (bf16[2,96,2,256]{3,1,2,0:T(8,128)(2,1)S(1)}, bf16[2,96,2,256]{3,1,2,0:T(8,128)(2,1)S(1)}, u32[]{:S(2)}, u32[]{:S(2)}) collective-permute-start(bf16[2,96,2,256]{3,1,2,0:T(8,128)(2,1)S(1)} %slice.888), channel_id=1, source_target_pairs={{0,64},{64,128},{128,192},{192,256},{256,320},{320,384},{384,448},... | collective-permute-start | bytes 589832 | tf_op jit(solution)/shard_map/ppermute | solution.py:12
  11.3 9.5 %collective-permute-start.1 = (bf16[6,96,1,256]{3,1,2,0:T(8,128)(2,1)S(1)}, bf16[6,96,1,256]{3,1,2,0:T(8,128)(2,1)S(1)}, u32[]{:S(2)}, u32[]{:S(2)}) collective-permute-start(bf16[6,96,1,256]{3,1,2,0:T(8,128)(2,1)S(1)} %get-tuple-element.239), channel_id=1, source_target_pairs={{0,1},{1,2},{2,3},{3,4},{4,5},{5,6},{6,7},{7,8},{8,9},{9,10},{10,1... | collective-permute-start | bytes 884744 | tf_op jit(solution)/shard_map/ppermute | solution.py:23
  17.1 9.3 %collective-permute-start.2 = (bf16[6,96,1,256]{3,1,2,0:T(8,128)(2,1)S(1)}, bf16[6,96,1,256]{3,1,2,0:T(8,128)(2,1)S(1)}, u32[]{:S(2)}, u32[]{:S(2)}) collective-permute-start(bf16[6,96,1,256]{3,1,2,0:T(8,128)(2,1)S(1)} %get-tuple-element.240), channel_id=1, source_target_pairs={{1,0},{2,1},{3,2},{4,3},{5,4},{6,5},{7,6},{8,7},{9,8},{10,9},{11,1... | collective-permute-start | bytes 884744 | tf_op jit(solution)/shard_map/ppermute | solution.py:25
  27.5 41.0 %copy-start.2 = (f32[96]{0:T(128)S(1)}, f32[96]{0:T(128)}, u32[]{:S(2)}) copy-start(f32[96]{0:T(128)} %param.12) | copy-start | bytes 1156
  33.8 0.9 copy-start
  43.7 0.9 copy-start
  53.7 0.9 copy-start
  63.6 0.9 copy-start
  70.0 7.9 %collective-permute-start.3 = (bf16[2,96,2,256]{3,1,2,0:T(8,128)(2,1)S(1)}, bf16[2,96,2,256]{3,1,2,0:T(8,128)(2,1)S(1)}, u32[]{:S(2)}, u32[]{:S(2)}) collective-permute-start(bf16[2,96,2,256]{3,1,2,0:T(8,128)(2,1)S(1)} %slice.891), channel_id=1, source_target_pairs={{0,64},{64,128},{128,192},{192,256},{256,320},{320,384},{384,448},... | collective-permute-start | bytes 589832 | tf_op jit(solution)/shard_map/ppermute | solution.py:12
  77.9 7.1 %collective-permute-start.4 = (bf16[6,96,1,256]{3,1,2,0:T(8,128)(2,1)S(1)}, bf16[6,96,1,256]{3,1,2,0:T(8,128)(2,1)S(1)}, u32[]{:S(2)}, u32[]{:S(2)}) collective-permute-start(bf16[6,96,1,256]{3,1,2,0:T(8,128)(2,1)S(1)} %get-tuple-element.237), channel_id=1, source_target_pairs={{0,1},{1,2},{2,3},{3,4},{4,5},{5,6},{6,7},{7,8},{8,9},{9,10},{10,1... | collective-permute-start | bytes 884744 | tf_op jit(solution)/shard_map/ppermute | solution.py:23
  81.4 9.3 %collective-permute-start.5 = (bf16[6,96,1,256]{3,1,2,0:T(8,128)(2,1)S(1)}, bf16[6,96,1,256]{3,1,2,0:T(8,128)(2,1)S(1)}, u32[]{:S(2)}, u32[]{:S(2)}) collective-permute-start(bf16[6,96,1,256]{3,1,2,0:T(8,128)(2,1)S(1)} %get-tuple-element.238), channel_id=1, source_target_pairs={{1,0},{2,1},{3,2},{4,3},{5,4},{6,5},{7,6},{8,7},{9,8},{10,9},{11,1... | collective-permute-start | bytes 884744 | tf_op jit(solution)/shard_map/ppermute | solution.py:25
  98.1 0.9 copy-start.1
  108.0 0.9 copy-start.1
  117.9 0.9 copy-start.1
  127.9 0.9 copy-start.1
where the time goes:
time: 136 us; the launch traced here: 134 us
  local copies, waits for them, and re-layouts  29.5 us (22%)
  starting transfers between devices  23.7 us (17%)
  matrix products  22.7 us (17%)
  waiting for transfers between devices  20.8 us (15%)
  other arithmetic  20.7 us (15%)
  loops' own time  16.6 us (12%)
    dot_general x72, matrix products, one_frame(): jnp.einsum('oc,chw->ohw', stacked, window, preferred_element_type=jnp.flo...  22.7 us
    another operation x2, loops' own time, conv_valid(): return lax.map(one_frame, jnp.arange(frames_out, dtype=jnp.int32))  16.6 us
    slice x8, local copies, waits for them, and re-layouts, one_frame(): stacked = kernel[tap_time, tap_row].reshape(3 * out_chan, in_chan)  15.1 us
    dynamic_update_slice x8, other arithmetic, conv_valid(): return lax.map(one_frame, jnp.arange(frames_out, dtype=jnp.int32))  13.9 us
    ppermute x2, waiting for transfers between devices, padded(): lax.ppermute(head, axis, [((i + 1) % count, i) for i in range(ends)])  11.2 us
    ppermute x2, starting transfers between devices, shifted(): return lax.ppermute(value, axis, pairs)  10.5 us
    ppermute x2, starting transfers between devices, padded(): lax.ppermute(tail, axis, [(i, (i + 1) % count) for i in range(ends)])  9.33 us
    ppermute x2, waiting for transfers between devices, shifted(): return lax.ppermute(value, axis, pairs)  6.14 us
  transfers between devices with their start and end apart: 6, of which 6 were waited for; matrix products, arithmetic and copies ran while one was open for 0% of the time, Pallas kernels for 0%

commit v1 on v0

v1 whole, which is shorter than its diff:
```python
import functools

import jax
import jax.numpy as jnp
from jax import lax
from jax.experimental import pallas as pl
from jax.experimental.pallas import tpu as pltpu
from jax.sharding import PartitionSpec as P

MESH = pl.DeviceIdType.MESH
epsilon = 1e-06


def norm_silu(values, gain):
    mean_square = jnp.mean(values * values, axis=0, keepdims=True)
    v = values * lax.rsqrt(mean_square + epsilon) * gain
    return (v / (1.0 + jnp.exp(-v))).astype(jnp.bfloat16)


def stack_taps(taps, stacked):
    chan = taps.shape[-1]
    for e in range(3):
        stacked[chan * e : chan * (e + 1), :] = jnp.concatenate(
            [taps[a, b, e] for a in range(3) for b in range(3)], axis=1
        )


def as_column(row):
    chan = row.shape[0]
    wide = jnp.broadcast_to(row[None, :], (chan, chan))
    i = lax.broadcasted_iota(jnp.int32, (chan, chan), 0)
    j = lax.broadcasted_iota(jnp.int32, (chan, chan), 1)
    return jnp.sum(jnp.where(i == j, wide, 0.0), axis=1, keepdims=True)


def conv_row(cells, stacked, frame, row):
    chan, width = cells.shape[2], cells.shape[3]
    window = jnp.concatenate(
        [
            cells[frame - 2 + a, pl.ds(row, 3)].reshape(3 * chan, width)
            for a in range(3)
        ],
        axis=0,
    )
    p = jnp.dot(stacked[...], window, preferred_element_type=jnp.float32)
    column = lax.broadcasted_iota(jnp.int32, (chan, width), 1)
    before = jnp.where(column == 0, 0.0, pltpu.roll(p[:chan], 1, 1))
    after = jnp.where(
        column == width - 1, 0.0, pltpu.roll(p[2 * chan :], width - 1, 1)
    )
    return before + p[chan : 2 * chan] + after


def kernel(
    tm, rows, feat_hbm, gain1_hbm, taps1_hbm, gain2_hbm, taps2_hbm, out_hbm,
    feat, gain1, gain2, taps1, taps2, stack1, stack2, ext1, ext2, out,
    load_sem, store_sem, send_sem, recv_sem,
):
    t = lax.axis_index("tm")
    r = lax.axis_index("rows")
    core = lax.rem(r, 2)
    chan, width = feat.shape[1], feat.shape[3]
    last = feat.shape[0] + 2

    outer_at = r - 1 + 2 * core
    has_outer = jnp.logical_and(outer_at >= 0, outer_at < rows)
    outer = (t, jnp.clip(outer_at, 0, rows - 1))
    inner = (t, r + 1 - 2 * core)
    has_next = t < tm - 1
    has_prev = t > 0
    after = (jnp.minimum(t + 1, tm - 1), r)
    before = (jnp.maximum(t - 1, 0), r)
    own_outer, own_inner = 1 + core, 2 - core
    to_outer, to_inner = 3 - 3 * core, 3 * core

    barrier = pltpu.get_barrier_semaphore()
    pl.semaphore_signal(barrier, inc=1, device_id=inner, device_id_type=MESH)

    @pl.when(has_outer)
    def _():
        pl.semaphore_signal(barrier, inc=1, device_id=outer, device_id_type=MESH)

    @pl.when(has_prev)
    def _():
        pl.semaphore_signal(barrier, inc=1, device_id=before, device_id_type=MESH)

    order = (3, 2, 1, 0)
    feat_in = {
        f: pltpu.make_async_copy(feat_hbm.at[f], feat.at[f], load_sem.at[f])
        for f in order
    }
    rest_in = [
        pltpu.make_async_copy(src, dst, load_sem.at[4 + i])
        for i, (src, dst) in enumerate(
            ((gain1_hbm, gain1), (gain2_hbm, gain2), (taps1_hbm, taps1), (taps2_hbm, taps2))
        )
    ]
    rest_in[0].start()
    for f in order:
        feat_in[f].start()
    for copy in rest_in[1:]:
        copy.start()

    def remote(ext, n, src_frames, src_row, dst_frames, dst_row, device):
        return pltpu.make_async_remote_copy(
            src_ref=ext.at[src_frames, src_row],
            dst_ref=ext.at[dst_frames, dst_row],
            send_sem=send_sem.at[n],
            recv_sem=recv_sem.at[n],
            device_id=device,
            device_id_type=MESH,
        )

    def transfers(ext, n, cut):
        late, early = slice(cut, last), slice(2, cut)
        tail, head = slice(last - 2, last), slice(0, 2)
        return dict(
            z_outer=remote(ext, n, tail, own_outer, head, own_outer, after),
            z_inner=remote(ext, n + 1, tail, own_inner, head, own_inner, after),
            outer_late=remote(ext, n + 2, late, own_outer, late, to_outer, outer),
            outer_early=remote(ext, n + 3, early, own_outer, early, to_outer, outer),
            inner_late=remote(ext, n + 4, late, own_inner, late, to_inner, inner),
            inner_early=remote(ext, n + 5, early, own_inner, early, to_inner, inner),
            relay_outer=remote(ext, n + 6, head, own_outer, head, to_outer, outer),
            relay_inner=remote(ext, n + 7, head, own_inner, head, to_inner, inner),
        )

    moves1 = transfers(ext1, 0, 3)
    moves2 = transfers(ext2, 8, 4)
    both = jnp.logical_and(has_prev, has_outer)
    sends_if = dict(
        z_outer=has_next, z_inner=has_next, outer_late=has_outer, outer_early=has_outer,
        inner_late=None, inner_early=None, relay_outer=both, relay_inner=has_prev,
    )
    gets_if = dict(sends_if, z_outer=has_prev, z_inner=has_prev)

    def when(condition, action):
        if condition is None:
            action()
        else:
            pl.when(condition)(action)

    def send(moves, *names):
        for name in names:
            when(sends_if[name], moves[name].start)

    def got(moves, *names):
        for name in names:
            when(gets_if[name], moves[name].wait_recv)

    zero_row = jnp.zeros((chan, width), jnp.bfloat16)

    @pl.when(t == 0)
    def _():
        for ext in (ext1, ext2):
            for f in range(2):
                for row in range(4):
                    ext[f, row] = zero_row

    @pl.when(jnp.logical_not(has_outer))
    def _():
        for ext in (ext1, ext2):
            for f in range(last):
                ext[f, 3 * core] = zero_row

    rest_in[0].wait()
    column1 = as_column(gain1[...])

    def first(f):
        feat_in[f].wait()
        x = feat[f].astype(jnp.float32).reshape(chan, 2 * width)
        for row in range(2):
            ext1[2 + f, 1 + row] = norm_silu(x[:, row * width : (row + 1) * width], column1)

    first(3)
    first(2)
    neighbours = 1 + has_outer.astype(jnp.int32) + has_next.astype(jnp.int32)
    pl.semaphore_wait(barrier, neighbours)
    send(moves1, "z_outer", "z_inner")
    first(1)
    send(moves1, "outer_late", "inner_late")
    first(0)
    send(moves1, "outer_early", "inner_early")

    for copy in rest_in[1:]:
        copy.wait()
    stack_taps(taps1, stack1)
    column2 = as_column(gain2[...])

    def hidden(frame, row):
        return norm_silu(conv_row(ext1, stack1, frame, row), column2)

    got(moves1, "inner_late", "inner_early")
    for frame in (5, 4):
        ext2[frame, own_inner] = hidden(frame, 1 - core)
    stack_taps(taps2, stack2)
    got(moves1, "outer_late", "outer_early")
    for frame in (5, 4):
        ext2[frame, own_outer] = hidden(frame, core)
    send(moves2, "z_outer", "z_inner", "outer_late", "inner_late")
    got(moves1, "z_outer")
    send(moves1, "relay_outer")
    got(moves1, "z_inner")
    send(moves1, "relay_inner")
    got(moves1, "relay_outer", "relay_inner")
    for frame in (3, 2):
        for row in range(2):
            ext2[frame, 1 + row] = hidden(frame, row)
    send(moves2, "outer_early", "inner_early")

    def decoded(frame):
        mixed = jnp.concatenate(
            [conv_row(ext2, stack2, frame, row) for row in range(2)], axis=1
        )
        x = feat[frame - 2].astype(jnp.float32).reshape(chan, 2 * width)
        out[frame - 2] = (mixed + x).reshape(chan, 2, width).astype(jnp.bfloat16)
        copy = pltpu.make_async_copy(
            out.at[frame - 2], out_hbm.at[frame - 2], store_sem.at[frame - 2]
        )
        copy.start()
        return copy

    got(moves2, "z_outer")
    send(moves2, "relay_outer")
    got(moves2, "outer_late", "inner_late", "outer_early", "inner_early")
    stores = [decoded(5), decoded(4)]
    got(moves2, "z_inner")
    send(moves2, "relay_inner")
    got(moves2, "relay_outer", "relay_inner")
    stores += [decoded(3), decoded(2)]

    for moves in (moves1, moves2):
        for name, move in moves.items():
            when(sends_if[name], move.wait_send)
    for copy in stores:
        copy.wait()


def on_device(tm, rows, features, gain_first, conv_first, gain_second, conv_second):
    frames, chan, height, width = features.shape
    ext = pltpu.VMEM((frames + 2, height + 2, chan, width), jnp.bfloat16)
    stack = pltpu.VMEM((3 * chan, 9 * chan), jnp.bfloat16)
    return pl.pallas_call(
        functools.partial(kernel, tm, rows),
        out_shape=jax.ShapeDtypeStruct(features.shape, features.dtype),
        in_specs=[pl.BlockSpec(memory_space=pl.ANY)] * 5,
        out_specs=pl.BlockSpec(memory_space=pl.ANY),
        scratch_shapes=[
            pltpu.VMEM(features.shape, features.dtype),
            pltpu.VMEM(gain_first.shape, gain_first.dtype),
            pltpu.VMEM(gain_second.shape, gain_second.dtype),
            pltpu.VMEM(conv_first.shape, conv_first.dtype),
            pltpu.VMEM(conv_second.shape, conv_second.dtype),
            stack,
            stack,
            ext,
            ext,
            pltpu.VMEM(features.shape, features.dtype),
            pltpu.SemaphoreType.DMA((8,)),
            pltpu.SemaphoreType.DMA((4,)),
            pltpu.SemaphoreType.DMA((16,)),
            pltpu.SemaphoreType.DMA((16,)),
        ],
        compiler_params=pltpu.CompilerParams(
            collective_id=0, has_side_effects=True, vmem_limit_bytes=60 << 20
        ),
        cost_estimate=pl.CostEstimate(
            flops=4 * 27 * chan * chan * frames * height * width,
            bytes_accessed=3 << 20,
            transcendentals=0,
        ),
        name="residual_block",
    )(features, gain_first, conv_first, gain_second, conv_second)


def solution(mesh):
    placed = (P("tm", None, "rows", None), P(), P(), P(), P())
    return jax.shard_map(
        functools.partial(on_device, mesh.shape["tm"], mesh.shape["rows"]),
        mesh=mesh,
        in_specs=placed,
        out_specs=P("tm", None, "rows", None),
        check_vma=False,
    )
```

time: 136 us -> 28.6 us (0.21)
  the two profiles are of different devices: /device:TPU:219 before, /device:TPU:199 now
where the time goes in v1:
time: 28.6 us; the launch traced here: 28.4 us
  Pallas kernels  26.4 us (92%)
  local copies, waits for them, and re-layouts  2.01 us (7%)
    pallas_call x1, Pallas kernels, on_device(): pl.pallas_call(functools.partial(kernel, tm, rows), out_shape=jax.ShapeDt...  26.4 us
    unnamed x1, local copies, waits for them, and re-layouts  2.01 us

profile of v1, /device:TPU:199, one launch (start us, length us, event | category | flops | bytes accessed | tf_op | source)
XLA Modules:
  0.0 28.4 jit_solution(2774329515211849561)
XLA Ops:
  0.0 26.4 %residual_block.1 = bf16[4,96,2,256]{3,2,1,0:T(2,128)(2,1)} custom-call(bf16[4,96,2,256]{3,2,1,0:T(2,128)(2,1)} %feat_hbm.1, f32[96]{0:T(128)} %gain1_hbm.1, bf16[3,3,3,96,96]{4,3,2,1,0:T(8,128)(2,1)} %taps1_hbm.1, f32[96]{0:T(128)} %gain2_hbm.1, bf16[3,3,3,96,96]{4,3,2,1,0:T(8,128)(2,1)} %taps2_hbm.1), custom_call_target="tpu_custom_call" | custom-call | flops 2038431744 | bytes 3145728 | tf_op jit(solution)/shard_map/residual_block/pallas_call | solution.py:243
  26.4 2.0 %copy.7 = bf16[4,96,2,256]{3,2,1,0:T(2,128)(2,1)} copy(bf16[4,96,2,256]{3,2,1,0:T(2,128)(2,1)} %residual_block.1) | data formatting | bytes 786432

commit v2 on v1

v2 whole, which is shorter than its diff:
```python
import functools

import jax
import jax.numpy as jnp
from jax import lax
from jax.experimental import pallas as pl
from jax.experimental.pallas import tpu as pltpu
from jax.sharding import PartitionSpec as P

MESH = pl.DeviceIdType.MESH
epsilon = 1e-06


def norm_silu(values, gain):
    mean_square = jnp.mean(values * values, axis=0, keepdims=True)
    v = values * lax.rsqrt(mean_square + epsilon) * gain
    return (v / (1.0 + jnp.exp(-v))).astype(jnp.bfloat16)


def stack_taps(taps, own, edge):
    chan = taps.shape[-1]
    for row, (inside, beyond) in enumerate((((1, 2), 0), ((0, 1), 2))):
        for e in range(3):
            span = slice(chan * e, chan * (e + 1))
            own[row, span, :] = jnp.concatenate(
                [taps[a, b, e] for a in range(3) for b in inside], axis=1
            )
            edge[row, span, :] = jnp.concatenate(
                [taps[a, beyond, e] for a in range(3)], axis=1
            )


def as_column(row):
    chan = row.shape[0]
    wide = jnp.broadcast_to(row[None, :], (chan, chan))
    i = lax.broadcasted_iota(jnp.int32, (chan, chan), 0)
    j = lax.broadcasted_iota(jnp.int32, (chan, chan), 1)
    return jnp.sum(jnp.where(i == j, wide, 0.0), axis=1, keepdims=True)


def from_own(cells, stacked, frame, row):
    chan, width = cells.shape[2], cells.shape[3]
    window = [
        cells[frame - 2 + a, 1:3].reshape(2 * chan, width) for a in range(3)
    ]
    return jnp.dot(
        stacked[row], jnp.concatenate(window, axis=0), preferred_element_type=jnp.float32
    )


def from_edge(cells, stacked, frame, row):
    window = [cells[frame - 2 + a, 3 * row] for a in range(3)]
    return jnp.dot(
        stacked[row], jnp.concatenate(window, axis=0), preferred_element_type=jnp.float32
    )


def gather_columns(p):
    chan, width = p.shape[0] // 3, p.shape[1]
    column = lax.broadcasted_iota(jnp.int32, (chan, width), 1)
    before = jnp.where(column == 0, 0.0, pltpu.roll(p[:chan], 1, 1))
    after = jnp.where(
        column == width - 1, 0.0, pltpu.roll(p[2 * chan :], width - 1, 1)
    )
    return before + p[chan : 2 * chan] + after


def kernel(
    tm, rows, feat_hbm, gain1_hbm, taps1_hbm, gain2_hbm, taps2_hbm, out_hbm,
    feat, gain1, gain2, taps1, taps2, own1, edge1, own2, edge2, ext1, ext2, part, mixed, out,
    load_sem, store_sem, send_sem, recv_sem,
):
    t = lax.axis_index("tm")
    r = lax.axis_index("rows")
    core = lax.rem(r, 2)
    chan, width = feat.shape[1], feat.shape[3]
    last = feat.shape[0] + 2

    outer_at = r - 1 + 2 * core
    has_outer = jnp.logical_and(outer_at >= 0, outer_at < rows)
    outer = (t, jnp.clip(outer_at, 0, rows - 1))
    inner = (t, r + 1 - 2 * core)
    has_next = t < tm - 1
    has_prev = t > 0
    after = (jnp.minimum(t + 1, tm - 1), r)
    before = (jnp.maximum(t - 1, 0), r)
    own_outer, own_inner = 1 + core, 2 - core
    to_outer, to_inner = 3 - 3 * core, 3 * core

    barrier = pltpu.get_barrier_semaphore()
    pl.semaphore_signal(barrier, inc=1, device_id=inner, device_id_type=MESH)

    @pl.when(has_outer)
    def _():
        pl.semaphore_signal(barrier, inc=1, device_id=outer, device_id_type=MESH)

    @pl.when(has_prev)
    def _():
        pl.semaphore_signal(barrier, inc=1, device_id=before, device_id_type=MESH)

    order = (3, 2, 1, 0)
    feat_in = {
        f: pltpu.make_async_copy(feat_hbm.at[f], feat.at[f], load_sem.at[f])
        for f in order
    }
    rest_in = [
        pltpu.make_async_copy(src, dst, load_sem.at[4 + i])
        for i, (src, dst) in enumerate(
            ((gain1_hbm, gain1), (gain2_hbm, gain2), (taps1_hbm, taps1), (taps2_hbm, taps2))
        )
    ]
    rest_in[0].start()
    for f in order:
        feat_in[f].start()
    for copy in rest_in[1:]:
        copy.start()

    def remote(ext, n, src_frames, src_row, dst_frames, dst_row, device):
        return pltpu.make_async_remote_copy(
            src_ref=ext.at[src_frames, src_row],
            dst_ref=ext.at[dst_frames, dst_row],
            send_sem=send_sem.at[n],
            recv_sem=recv_sem.at[n],
            device_id=device,
            device_id_type=MESH,
        )

    both = jnp.logical_and(has_prev, has_outer)
    moves = {}

    def plan_z(name, ext, row, cuts):
        for i, (low, high) in enumerate(cuts):
            moves[name, i] = (
                remote(ext, len(moves), slice(low + 4, high + 4), row, slice(low, high), row, after),
                has_next,
                has_prev,
            )

    def plan_rows(name, ext, cuts, relayed=False):
        for i, (low, high) in enumerate(cuts):
            frames = slice(low, high)
            condition = both if relayed else has_outer
            moves[name + "_outer", i] = (
                remote(ext, len(moves), frames, own_outer, frames, to_outer, outer),
                condition,
                condition,
            )
            condition = has_prev if relayed else None
            moves[name + "_inner", i] = (
                remote(ext, len(moves), frames, own_inner, frames, to_inner, inner),
                condition,
                condition,
            )

    plan_z("z1_outer", ext1, own_outer, ((0, 1), (1, 2)))
    plan_z("z1_inner", ext1, own_inner, ((0, 2),))
    plan_rows("late1", ext1, ((3, 6),))
    plan_rows("early1", ext1, ((2, 3),))
    plan_rows("relay1", ext1, ((0, 1), (1, 2)), True)
    plan_z("z2_outer", ext2, own_outer, ((0, 1), (1, 2)))
    plan_z("z2_inner", ext2, own_inner, ((0, 2),))
    plan_rows("late2", ext2, ((4, 6),))
    plan_rows("early2", ext2, ((2, 4),))
    plan_rows("relay2", ext2, ((0, 1), (1, 2)), True)

    def when(condition, action):
        if condition is None:
            action()
        else:
            pl.when(condition)(action)

    def send(name, i=0):
        copy, sends, _ = moves[name, i]
        when(sends, copy.start)

    def got(name, i=0):
        copy, _, gets = moves[name, i]
        when(gets, copy.wait_recv)

    zero_row = jnp.zeros((chan, width), jnp.bfloat16)

    @pl.when(t == 0)
    def _():
        for ext in (ext1, ext2):
            for f in range(2):
                for row in range(4):
                    ext[f, row] = zero_row

    @pl.when(jnp.logical_not(has_outer))
    def _():
        for ext in (ext1, ext2):
            for f in range(last):
                ext[f, 3 * core] = zero_row

    rest_in[0].wait()
    column1 = as_column(gain1[...])

    def first(f):
        feat_in[f].wait()
        x = feat[f].astype(jnp.float32).reshape(chan, 2 * width)
        for row in range(2):
            ext1[2 + f, 1 + row] = norm_silu(x[:, row * width : (row + 1) * width], column1)

    first(3)
    first(2)
    neighbours = 1 + has_outer.astype(jnp.int32) + has_next.astype(jnp.int32)
    pl.semaphore_wait(barrier, neighbours)
    for i in (0, 1):
        send("z1_outer", i)
    first(1)
    send("late1_outer")
    send("late1_inner")
    first(0)
    send("early1_outer")
    send("early1_inner")

    out_outer, out_inner = core, 1 - core

    def start1(frame):
        for row in range(2):
            part[frame - 2, row] = from_own(ext1, own1, frame, row)

    def second(frame, row):
        p = part[frame - 2, row] + from_edge(ext1, edge1, frame, row)
        ext2[frame, 1 + row] = norm_silu(gather_columns(p), column2)

    for copy in rest_in[1:]:
        copy.wait()
    stack_taps(taps1, own1, edge1)
    column2 = as_column(gain2[...])
    start1(5)
    start1(4)
    send("z1_inner")
    got("late1_inner")
    got("early1_inner")
    second(5, out_inner)
    second(4, out_inner)
    stack_taps(taps2, own2, edge2)
    got("z1_outer", 0)
    send("relay1_outer", 0)
    got("late1_outer")
    second(5, out_outer)
    send("z2_outer", 1)
    got("z1_outer", 1)
    send("relay1_outer", 1)
    got("early1_outer")
    second(4, out_outer)
    send("z2_outer", 0)
    send("late2_outer")
    send("late2_inner")
    got("z1_inner")
    for i in range(2):
        send("relay1_inner", i)
    send("z2_inner")
    start1(3)
    start1(2)
    for i in range(2):
        got("relay1_outer", i)
    second(3, out_outer)
    second(2, out_outer)
    send("early2_outer")
    for i in range(2):
        got("relay1_inner", i)
    second(3, out_inner)
    second(2, out_inner)
    send("early2_inner")

    def start2(frame):
        for row in range(2):
            part[frame - 2, row] = from_own(ext2, own2, frame, row)

    def mix(frame, row):
        p = part[frame - 2, row] + from_edge(ext2, edge2, frame, row)
        mixed[frame - 2, row] = gather_columns(p)

    stores = []

    def finish(frame):
        x = feat[frame - 2].astype(jnp.float32).reshape(chan, 2 * width)
        total = jnp.concatenate([mixed[frame - 2, 0], mixed[frame - 2, 1]], axis=1) + x
        out[frame - 2] = total.reshape(chan, 2, width).astype(jnp.bfloat16)
        copy = pltpu.make_async_copy(
            out.at[frame - 2], out_hbm.at[frame - 2], store_sem.at[frame - 2]
        )
        copy.start()
        stores.append(copy)

    for i in (1, 0):
        got("z2_outer", i)
        send("relay2_outer", i)
    start2(5)
    start2(4)
    got("late2_inner")
    got("early2_inner")
    mix(5, out_inner)
    mix(4, out_inner)
    got("z2_inner")
    for i in range(2):
        send("relay2_inner", i)
    start2(3)
    start2(2)
    got("late2_outer")
    got("early2_outer")
    mix(5, out_outer)
    mix(4, out_outer)
    finish(5)
    finish(4)
    for i in range(2):
        got("relay2_outer", i)
    mix(3, out_outer)
    mix(2, out_outer)
    for i in range(2):
        got("relay2_inner", i)
    mix(3, out_inner)
    mix(2, out_inner)
    finish(3)
    finish(2)

    for copy, sends, _ in moves.values():
        when(sends, copy.wait_send)
    for copy in stores:
        copy.wait()


def on_device(tm, rows, features, gain_first, conv_first, gain_second, conv_second):
    frames, chan, height, width = features.shape
    ext = pltpu.VMEM((frames + 2, height + 2, chan, width), jnp.bfloat16)
    own = pltpu.VMEM((2, 3 * chan, 6 * chan), jnp.bfloat16)
    edge = pltpu.VMEM((2, 3 * chan, 3 * chan), jnp.bfloat16)
    return pl.pallas_call(
        functools.partial(kernel, tm, rows),
        out_shape=jax.ShapeDtypeStruct(features.shape, features.dtype),
        in_specs=[pl.BlockSpec(memory_space=pl.ANY)] * 5,
        out_specs=pl.BlockSpec(memory_space=pl.ANY),
        scratch_shapes=[
            pltpu.VMEM(features.shape, features.dtype),
            pltpu.VMEM(gain_first.shape, gain_first.dtype),
            pltpu.VMEM(gain_second.shape, gain_second.dtype),
            pltpu.VMEM(conv_first.shape, conv_first.dtype),
            pltpu.VMEM(conv_second.shape, conv_second.dtype),
            own,
            edge,
            own,
            edge,
            ext,
            ext,
            pltpu.VMEM((frames, height, 3 * chan, width), jnp.float32),
            pltpu.VMEM((frames, height, chan, width), jnp.float32),
            pltpu.VMEM(features.shape, features.dtype),
            pltpu.SemaphoreType.DMA((8,)),
            pltpu.SemaphoreType.DMA((4,)),
            pltpu.SemaphoreType.DMA((32,)),
            pltpu.SemaphoreType.DMA((32,)),
        ],
        compiler_params=pltpu.CompilerParams(
            collective_id=0, has_side_effects=True, vmem_limit_bytes=60 << 20
        ),
        cost_estimate=pl.CostEstimate(
            flops=4 * 27 * chan * chan * frames * height * width,
            bytes_accessed=3 << 20,
            transcendentals=0,
        ),
        name="residual_block",
    )(features, gain_first, conv_first, gain_second, conv_second)


def solution(mesh):
    placed = (P("tm", None, "rows", None), P(), P(), P(), P())
    return jax.shard_map(
        functools.partial(on_device, mesh.shape["tm"], mesh.shape["rows"]),
        mesh=mesh,
        in_specs=placed,
        out_specs=P("tm", None, "rows", None),
        check_vma=False,
    )
```

time: 28.6 us -> 24.7 us (0.86)
  the two profiles are of different devices: /device:TPU:199 before, /device:TPU:198 now
where the time goes in v2:
time: 24.7 us; the launch traced here: 24.5 us
  Pallas kernels  22.5 us (91%)
  local copies, waits for them, and re-layouts  2.01 us (8%)
    pallas_call x1, Pallas kernels, on_device(): pl.pallas_call(functools.partial(kernel, tm, rows), out_shape=jax.ShapeDt...  22.5 us
    unnamed x1, local copies, waits for them, and re-layouts  2.01 us

profile of v2, /device:TPU:198, one launch (start us, length us, event | category | flops | bytes accessed | tf_op | source)
XLA Modules:
  0.0 24.5 jit_solution(2684524195669116400)
XLA Ops:
  0.0 22.5 %residual_block.1 = bf16[4,96,2,256]{3,2,1,0:T(2,128)(2,1)} custom-call(bf16[4,96,2,256]{3,2,1,0:T(2,128)(2,1)} %feat_hbm.1, f32[96]{0:T(128)} %gain1_hbm.1, bf16[3,3,3,96,96]{4,3,2,1,0:T(8,128)(2,1)} %taps1_hbm.1, f32[96]{0:T(128)} %gain2_hbm.1, bf16[3,3,3,96,96]{4,3,2,1,0:T(8,128)(2,1)} %taps2_hbm.1), custom_call_target="tpu_custom_call" | custom-call | flops 2038431744 | bytes 3145728 | tf_op jit(solution)/shard_map/residual_block/pallas_call | solution.py:330
  22.5 2.0 %copy.7 = bf16[4,96,2,256]{3,2,1,0:T(2,128)(2,1)} copy(bf16[4,96,2,256]{3,2,1,0:T(2,128)(2,1)} %residual_block.1) | data formatting | bytes 786432

commit v3 on v2

--- a/solution.py
+++ b/solution.py
@@ -19,15 +19,17 @@
 
 def stack_taps(taps, own, edge):
     chan = taps.shape[-1]
+    depth = own.shape[-1]
     for row, (inside, beyond) in enumerate((((1, 2), 0), ((0, 1), 2))):
         for e in range(3):
             span = slice(chan * e, chan * (e + 1))
-            own[row, span, :] = jnp.concatenate(
-                [taps[a, b, e] for a in range(3) for b in inside], axis=1
+            wide = jnp.concatenate(
+                [taps[a, b, e] for a in range(3) for b in inside]
+                + [taps[a, beyond, e] for a in range(3)],
+                axis=1,
             )
-            edge[row, span, :] = jnp.concatenate(
-                [taps[a, beyond, e] for a in range(3)], axis=1
-            )
+            own[row, span, :] = wide[:, :depth]
+            edge[row, span, :] = wide[:, depth:]
 
 
 def as_column(row):
@@ -41,7 +43,10 @@
 def from_own(cells, stacked, frame, row):
     chan, width = cells.shape[2], cells.shape[3]
     window = [
-        cells[frame - 2 + a, 1:3].reshape(2 * chan, width) for a in range(3)
+        cells[frame - 2, 1:3].reshape(2 * chan, width),
+        cells[frame - 1, 1:3].reshape(2 * chan, width),
+        cells[frame, 1],
+        cells[frame, 2, : stacked.shape[-1] - 5 * chan],
     ]
     return jnp.dot(
         stacked[row], jnp.concatenate(window, axis=0), preferred_element_type=jnp.float32
@@ -49,7 +54,9 @@
 
 
 def from_edge(cells, stacked, frame, row):
-    window = [cells[frame - 2 + a, 3 * row] for a in range(3)]
+    chan = cells.shape[2]
+    window = [cells[frame, 2, 4 * chan - stacked.shape[-1] :]]
+    window += [cells[frame - 2 + a, 3 * row] for a in range(3)]
     return jnp.dot(
         stacked[row], jnp.concatenate(window, axis=0), preferred_element_type=jnp.float32
     )
@@ -66,9 +73,9 @@
 
 
 def kernel(
-    tm, rows, feat_hbm, gain1_hbm, taps1_hbm, gain2_hbm, taps2_hbm, out_hbm,
-    feat, gain1, gain2, taps1, taps2, own1, edge1, own2, edge2, ext1, ext2, part, mixed, out,
-    load_sem, store_sem, send_sem, recv_sem,
+    tm, rows, feat_hbm, gain1_hbm, taps1_hbm, gain2_hbm, taps2_hbm, out,
+    feat, gain1, gain2, taps1, taps2, own1, edge1, own2, edge2, ext1, ext2, part, mixed,
+    load_sem, send_sem, recv_sem,
 ):
     t = lax.axis_index("tm")
     r = lax.axis_index("rows")
@@ -205,7 +212,7 @@
     first(2)
     neighbours = 1 + has_outer.astype(jnp.int32) + has_next.astype(jnp.int32)
     pl.semaphore_wait(barrier, neighbours)
-    for i in (0, 1):
+    for i in (1, 0):
         send("z1_outer", i)
     first(1)
     send("late1_outer")
@@ -273,17 +280,10 @@
         p = part[frame - 2, row] + from_edge(ext2, edge2, frame, row)
         mixed[frame - 2, row] = gather_columns(p)
 
-    stores = []
-
     def finish(frame):
         x = feat[frame - 2].astype(jnp.float32).reshape(chan, 2 * width)
         total = jnp.concatenate([mixed[frame - 2, 0], mixed[frame - 2, 1]], axis=1) + x
         out[frame - 2] = total.reshape(chan, 2, width).astype(jnp.bfloat16)
-        copy = pltpu.make_async_copy(
-            out.at[frame - 2], out_hbm.at[frame - 2], store_sem.at[frame - 2]
-        )
-        copy.start()
-        stores.append(copy)
 
     for i in (1, 0):
         got("z2_outer", i)
@@ -312,26 +312,27 @@
     for i in range(2):
         got("relay2_inner", i)
     mix(3, out_inner)
+    finish(3)
     mix(2, out_inner)
-    finish(3)
     finish(2)
 
     for copy, sends, _ in moves.values():
         when(sends, copy.wait_send)
-    for copy in stores:
-        copy.wait()
 
 
 def on_device(tm, rows, features, gain_first, conv_first, gain_second, conv_second):
     frames, chan, height, width = features.shape
     ext = pltpu.VMEM((frames + 2, height + 2, chan, width), jnp.bfloat16)
-    own = pltpu.VMEM((2, 3 * chan, 6 * chan), jnp.bfloat16)
-    edge = pltpu.VMEM((2, 3 * chan, 3 * chan), jnp.bfloat16)
+    depth = 6 * chan // 256 * 256
+    own = pltpu.VMEM((2, 3 * chan, depth), jnp.bfloat16)
+    edge = pltpu.VMEM((2, 3 * chan, 9 * chan - depth), jnp.bfloat16)
+    operands = (features, gain_first, conv_first, gain_second, conv_second)
+    operands = [pltpu.with_memory_space_constraint(x, pltpu.HBM) for x in operands]
     return pl.pallas_call(
         functools.partial(kernel, tm, rows),
-        out_shape=jax.ShapeDtypeStruct(features.shape, features.dtype),
+        out_shape=pltpu.VMEM(features.shape, features.dtype),
         in_specs=[pl.BlockSpec(memory_space=pl.ANY)] * 5,
-        out_specs=pl.BlockSpec(memory_space=pl.ANY),
+        out_specs=pl.BlockSpec(memory_space=pltpu.VMEM),
         scratch_shapes=[
             pltpu.VMEM(features.shape, features.dtype),
             pltpu.VMEM(gain_first.shape, gain_first.dtype),
@@ -346,14 +347,12 @@
             ext,
             pltpu.VMEM((frames, height, 3 * chan, width), jnp.float32),
             pltpu.VMEM((frames, height, chan, width), jnp.float32),
-            pltpu.VMEM(features.shape, features.dtype),
             pltpu.SemaphoreType.DMA((8,)),
-            pltpu.SemaphoreType.DMA((4,)),
-            pltpu.SemaphoreType.DMA((32,)),
-            pltpu.SemaphoreType.DMA((32,)),
+            pltpu.SemaphoreType.DMA((40,)),
+            pltpu.SemaphoreType.DMA((40,)),
         ],
         compiler_params=pltpu.CompilerParams(
-            collective_id=0, has_side_effects=True, vmem_limit_bytes=60 << 20
+            collective_id=0, has_side_effects=True, vmem_limit_bytes=32 << 20
         ),
         cost_estimate=pl.CostEstimate(
             flops=4 * 27 * chan * chan * frames * height * width,
@@ -361,7 +360,7 @@
             transcendentals=0,
         ),
         name="residual_block",
-    )(features, gain_first, conv_first, gain_second, conv_second)
+    )(*operands)
 
 
 def solution(mesh):

time: 24.7 us -> 22.9 us (0.927)
  local copies, waits for them, and re-layouts: 2.01 us -> 0.75 us
  Pallas kernels: 22.5 us -> 22 us
    unnamed x1, local copies, waits for them, and re-layouts: 2.01 us -> 0.75 us
    pallas_call x1, Pallas kernels: 22.5 us -> 22 us  [on_device(): pl.pallas_call(functools.partial(kernel, tm, rows), out_shape=pltpu.VMEM(...]
where the time goes in v3:
time: 22.9 us; the launch traced here: 22.7 us
  Pallas kernels  22 us (96%)
  local copies, waits for them, and re-layouts  0.75 us (3%)
    pallas_call x1, Pallas kernels, on_device(): pl.pallas_call(functools.partial(kernel, tm, rows), out_shape=pltpu.VMEM(...  22 us
    unnamed x1, local copies, waits for them, and re-layouts  0.75 us

profile of v3, /device:TPU:198, one launch (start us, length us, event | category | flops | bytes accessed | tf_op | source)
XLA Modules:
  0.0 22.7 jit_solution(4682477450993112605)
XLA Ops:
  0.0 22.0 %residual_block.1 = bf16[4,96,2,256]{3,2,1,0:T(2,128)(2,1)S(1)} custom-call(bf16[4,96,2,256]{3,2,1,0:T(2,128)(2,1)} %feat_hbm.1, f32[96]{0:T(128)} %gain1_hbm.1, bf16[3,3,3,96,96]{4,3,2,1,0:T(8,128)(2,1)} %taps1_hbm.1, f32[96]{0:T(128)} %gain2_hbm.1, bf16[3,3,3,96,96]{4,3,2,1,0:T(8,128)(2,1)} %taps2_hbm.1), custom_call_target="tpu_custom_call" | custom-call | flops 2038431744 | bytes 3145728 | tf_op jit(solution)/shard_map/residual_block/pallas_call | solution.py:331
  22.0 0.7 %copy.7 = bf16[4,96,2,256]{3,2,1,0:T(2,128)(2,1)} copy(bf16[4,96,2,256]{3,2,1,0:T(2,128)(2,1)S(1)} %residual_block.1) | data formatting | bytes 786432

commit v4 on v3

--- a/solution.py
+++ b/solution.py
@@ -159,16 +159,16 @@
                 condition,
             )
 
-    plan_z("z1_outer", ext1, own_outer, ((0, 1), (1, 2)))
+    halves = ((0, 1), (1, 2))
+    plan_z("z1_outer", ext1, own_outer, halves)
     plan_z("z1_inner", ext1, own_inner, ((0, 2),))
-    plan_rows("late1", ext1, ((3, 6),))
-    plan_rows("early1", ext1, ((2, 3),))
-    plan_rows("relay1", ext1, ((0, 1), (1, 2)), True)
-    plan_z("z2_outer", ext2, own_outer, ((0, 1), (1, 2)))
-    plan_z("z2_inner", ext2, own_inner, ((0, 2),))
+    plan_rows("rows1", ext1, ((2, 3), (3, 4), (4, 5), (5, 6)))
+    plan_rows("relay1", ext1, halves, True)
+    plan_z("z2_outer", ext2, own_outer, halves)
+    plan_z("z2_inner", ext2, own_inner, halves)
     plan_rows("late2", ext2, ((4, 6),))
-    plan_rows("early2", ext2, ((2, 4),))
-    plan_rows("relay2", ext2, ((0, 1), (1, 2)), True)
+    plan_rows("early2", ext2, ((2, 3), (3, 4)))
+    plan_rows("relay2", ext2, halves, True)
 
     def when(condition, action):
         if condition is None:
@@ -208,18 +208,15 @@
         for row in range(2):
             ext1[2 + f, 1 + row] = norm_silu(x[:, row * width : (row + 1) * width], column1)
 
-    first(3)
-    first(2)
     neighbours = 1 + has_outer.astype(jnp.int32) + has_next.astype(jnp.int32)
-    pl.semaphore_wait(barrier, neighbours)
-    for i in (1, 0):
-        send("z1_outer", i)
-    first(1)
-    send("late1_outer")
-    send("late1_inner")
-    first(0)
-    send("early1_outer")
-    send("early1_inner")
+    for f in order:
+        first(f)
+        if f == 3:
+            pl.semaphore_wait(barrier, neighbours)
+            send("z1_outer", 1)
+        send("rows1_outer", f)
+        send("rows1_inner", f)
+    send("z1_outer", 0)
 
     out_outer, out_inner = core, 1 - core
 
@@ -237,40 +234,48 @@
     column2 = as_column(gain2[...])
     start1(5)
     start1(4)
+    for f in order:
+        got("rows1_inner", f)
     send("z1_inner")
-    got("late1_inner")
-    got("early1_inner")
     second(5, out_inner)
     second(4, out_inner)
     stack_taps(taps2, own2, edge2)
+    got("z1_outer", 1)
+    send("relay1_outer", 1)
+    send("z2_inner", 1)
+    for f in order[:3]:
+        got("rows1_outer", f)
+    second(5, out_outer)
+    send("z2_outer", 1)
     got("z1_outer", 0)
     send("relay1_outer", 0)
-    got("late1_outer")
-    second(5, out_outer)
-    send("z2_outer", 1)
-    got("z1_outer", 1)
-    send("relay1_outer", 1)
-    got("early1_outer")
+    got("rows1_outer", 0)
     second(4, out_outer)
     send("z2_outer", 0)
     send("late2_outer")
     send("late2_inner")
     got("z1_inner")
-    for i in range(2):
+    for i in (1, 0):
         send("relay1_inner", i)
-    send("z2_inner")
+    send("z2_inner", 0)
     start1(3)
     start1(2)
-    for i in range(2):
-        got("relay1_outer", i)
+    got("relay1_outer", 1)
     second(3, out_outer)
+    send("early2_outer", 1)
+    got("relay1_outer", 0)
     second(2, out_outer)
-    send("early2_outer")
-    for i in range(2):
+    send("early2_outer", 0)
+    got("z2_inner", 1)
+    send("relay2_inner", 1)
+    for i in (1, 0):
         got("relay1_inner", i)
     second(3, out_inner)
     second(2, out_inner)
-    send("early2_inner")
+    for i in (1, 0):
+        send("early2_inner", i)
+    got("z2_outer", 1)
+    send("relay2_outer", 1)
 
     def start2(frame):
         for row in range(2):
@@ -285,35 +290,35 @@
         total = jnp.concatenate([mixed[frame - 2, 0], mixed[frame - 2, 1]], axis=1) + x
         out[frame - 2] = total.reshape(chan, 2, width).astype(jnp.bfloat16)
 
-    for i in (1, 0):
-        got("z2_outer", i)
-        send("relay2_outer", i)
     start2(5)
     start2(4)
+    got("z2_outer", 0)
+    send("relay2_outer", 0)
     got("late2_inner")
-    got("early2_inner")
+    for i in (1, 0):
+        got("early2_inner", i)
     mix(5, out_inner)
     mix(4, out_inner)
-    got("z2_inner")
-    for i in range(2):
-        send("relay2_inner", i)
     start2(3)
+    got("z2_inner", 0)
+    send("relay2_inner", 0)
     start2(2)
     got("late2_outer")
-    got("early2_outer")
+    for i in (1, 0):
+        got("early2_outer", i)
     mix(5, out_outer)
     mix(4, out_outer)
     finish(5)
     finish(4)
-    for i in range(2):
-        got("relay2_outer", i)
-    mix(3, out_outer)
-    mix(2, out_outer)
-    for i in range(2):
-        got("relay2_inner", i)
-    mix(3, out_inner)
+    got("relay2_outer", 1)
+    got("relay2_inner", 1)
+    mix(3, 0)
+    mix(3, 1)
     finish(3)
-    mix(2, out_inner)
+    got("relay2_outer", 0)
+    got("relay2_inner", 0)
+    mix(2, 0)
+    mix(2, 1)
     finish(2)
 
     for copy, sends, _ in moves.values():

time: 22.9 us -> 21.6 us (0.943)
  Pallas kernels: 22 us -> 20.7 us
    pallas_call x1, Pallas kernels: 22 us -> 20.7 us  [on_device(): pl.pallas_call(functools.partial(kernel, tm, rows), out_shape=pltpu.VMEM(...]
where the time goes in v4:
time: 21.6 us; the launch traced here: 21.5 us
  Pallas kernels  20.7 us (96%)
  local copies, waits for them, and re-layouts  0.75 us (3%)
    pallas_call x1, Pallas kernels, on_device(): pl.pallas_call(functools.partial(kernel, tm, rows), out_shape=pltpu.VMEM(...  20.7 us
    unnamed x1, local copies, waits for them, and re-layouts  0.75 us

profile of v4, /device:TPU:198, one launch (start us, length us, event | category | flops | bytes accessed | tf_op | source)
XLA Modules:
  0.0 21.5 jit_solution(12767426391987929548)
XLA Ops:
  0.0 20.7 %residual_block.1 = bf16[4,96,2,256]{3,2,1,0:T(2,128)(2,1)S(1)} custom-call(bf16[4,96,2,256]{3,2,1,0:T(2,128)(2,1)} %feat_hbm.1, f32[96]{0:T(128)} %gain1_hbm.1, bf16[3,3,3,96,96]{4,3,2,1,0:T(8,128)(2,1)} %taps1_hbm.1, f32[96]{0:T(128)} %gain2_hbm.1, bf16[3,3,3,96,96]{4,3,2,1,0:T(8,128)(2,1)} %taps2_hbm.1), custom_call_target="tpu_custom_call" | custom-call | flops 2038431744 | bytes 3145728 | tf_op jit(solution)/shard_map/residual_block/pallas_call | solution.py:336
  20.8 0.7 %copy.7 = bf16[4,96,2,256]{3,2,1,0:T(2,128)(2,1)} copy(bf16[4,96,2,256]{3,2,1,0:T(2,128)(2,1)S(1)} %residual_block.1) | data formatting | bytes 786432

commit v5 on v4

--- a/solution.py
+++ b/solution.py
@@ -245,12 +245,12 @@
     send("z2_inner", 1)
     for f in order[:3]:
         got("rows1_outer", f)
-    second(5, out_outer)
-    send("z2_outer", 1)
     got("z1_outer", 0)
     send("relay1_outer", 0)
     got("rows1_outer", 0)
+    second(5, out_outer)
     second(4, out_outer)
+    send("z2_outer", 1)
     send("z2_outer", 0)
     send("late2_outer")
     send("late2_inner")

time: 21.6 us -> 21.2 us (0.981)
  Pallas kernels: 20.7 us -> 20.3 us
    pallas_call x1, Pallas kernels: 20.7 us -> 20.3 us  [on_device(): pl.pallas_call(functools.partial(kernel, tm, rows), out_shape=pltpu.VMEM(...]
where the time goes in v5:
time: 21.2 us; the launch traced here: 21.1 us
  Pallas kernels  20.3 us (96%)
  local copies, waits for them, and re-layouts  0.75 us (4%)
    pallas_call x1, Pallas kernels, on_device(): pl.pallas_call(functools.partial(kernel, tm, rows), out_shape=pltpu.VMEM(...  20.3 us
    unnamed x1, local copies, waits for them, and re-layouts  0.75 us

profile of v5, /device:TPU:198, one launch (start us, length us, event | category | flops | bytes accessed | tf_op | source)
XLA Modules:
  0.0 21.1 jit_solution(7987301216688060694)
XLA Ops:
  0.0 20.3 %residual_block.1 = bf16[4,96,2,256]{3,2,1,0:T(2,128)(2,1)S(1)} custom-call(bf16[4,96,2,256]{3,2,1,0:T(2,128)(2,1)} %feat_hbm.1, f32[96]{0:T(128)} %gain1_hbm.1, bf16[3,3,3,96,96]{4,3,2,1,0:T(8,128)(2,1)} %taps1_hbm.1, f32[96]{0:T(128)} %gain2_hbm.1, bf16[3,3,3,96,96]{4,3,2,1,0:T(8,128)(2,1)} %taps2_hbm.1), custom_call_target="tpu_custom_call" | custom-call | flops 2038431744 | bytes 3145728 | tf_op jit(solution)/shard_map/residual_block/pallas_call | solution.py:336
  20.3 0.7 %copy.7 = bf16[4,96,2,256]{3,2,1,0:T(2,128)(2,1)} copy(bf16[4,96,2,256]{3,2,1,0:T(2,128)(2,1)S(1)} %residual_block.1) | data formatting | bytes 786432

commit v6 on v5

--- a/solution.py
+++ b/solution.py
@@ -184,6 +184,11 @@
         copy, _, gets = moves[name, i]
         when(gets, copy.wait_recv)
 
+    def sent(*names):
+        for (name, _), (copy, sends, _) in moves.items():
+            if name in names:
+                when(sends, copy.wait_send)
+
     zero_row = jnp.zeros((chan, width), jnp.bfloat16)
 
     @pl.when(t == 0)
@@ -217,6 +222,17 @@
         send("rows1_outer", f)
         send("rows1_inner", f)
     send("z1_outer", 0)
+
+    below = t == tm // 2 - 1
+
+    def pass_on(i):
+        got("z1_outer", i)
+        send("relay1_outer", i)
+
+    @pl.when(below)
+    def _():
+        pass_on(1)
+        pass_on(0)
 
     out_outer, out_inner = core, 1 - core
 
@@ -240,13 +256,11 @@
     second(5, out_inner)
     second(4, out_inner)
     stack_taps(taps2, own2, edge2)
-    got("z1_outer", 1)
-    send("relay1_outer", 1)
+    pl.when(jnp.logical_not(below))(functools.partial(pass_on, 1))
     send("z2_inner", 1)
     for f in order[:3]:
         got("rows1_outer", f)
-    got("z1_outer", 0)
-    send("relay1_outer", 0)
+    pl.when(jnp.logical_not(below))(functools.partial(pass_on, 0))
     got("rows1_outer", 0)
     second(5, out_outer)
     second(4, out_outer)
@@ -310,6 +324,7 @@
     mix(4, out_outer)
     finish(5)
     finish(4)
+    sent(*({name for name, _ in moves} - {"relay2_outer", "relay2_inner"}))
     got("relay2_outer", 1)
     got("relay2_inner", 1)
     mix(3, 0)
@@ -321,8 +336,7 @@
     mix(2, 1)
     finish(2)
 
-    for copy, sends, _ in moves.values():
-        when(sends, copy.wait_send)
+    sent("relay2_outer", "relay2_inner")
 
 
 def on_device(tm, rows, features, gain_first, conv_first, gain_second, conv_second):

time: 21.2 us -> 20 us (0.943)
  the two profiles are of different devices: /device:TPU:198 before, /device:TPU:134 now
where the time goes in v6:
time: 20 us; the launch traced here: 19.9 us
  Pallas kernels  19.1 us (96%)
  local copies, waits for them, and re-layouts  0.75 us (4%)
    pallas_call x1, Pallas kernels, on_device(): pl.pallas_call(functools.partial(kernel, tm, rows), out_shape=pltpu.VMEM(...  19.1 us
    unnamed x1, local copies, waits for them, and re-layouts  0.75 us

profile of v6, /device:TPU:134, one launch (start us, length us, event | category | flops | bytes accessed | tf_op | source)
XLA Modules:
  0.0 19.9 jit_solution(16647367147965150618)
XLA Ops:
  0.0 19.1 %residual_block.1 = bf16[4,96,2,256]{3,2,1,0:T(2,128)(2,1)S(1)} custom-call(bf16[4,96,2,256]{3,2,1,0:T(2,128)(2,1)} %feat_hbm.1, f32[96]{0:T(128)} %gain1_hbm.1, bf16[3,3,3,96,96]{4,3,2,1,0:T(8,128)(2,1)} %taps1_hbm.1, f32[96]{0:T(128)} %gain2_hbm.1, bf16[3,3,3,96,96]{4,3,2,1,0:T(8,128)(2,1)} %taps2_hbm.1), custom_call_target="tpu_custom_call" | custom-call | flops 2038431744 | bytes 3145728 | tf_op jit(solution)/shard_map/residual_block/pallas_call | solution.py:350
  19.1 0.7 %copy.7 = bf16[4,96,2,256]{3,2,1,0:T(2,128)(2,1)} copy(bf16[4,96,2,256]{3,2,1,0:T(2,128)(2,1)S(1)} %residual_block.1) | data formatting | bytes 786432

commit v7 on v6

--- a/solution.py
+++ b/solution.py
@@ -14,7 +14,8 @@
 def norm_silu(values, gain):
     mean_square = jnp.mean(values * values, axis=0, keepdims=True)
     v = values * lax.rsqrt(mean_square + epsilon) * gain
-    return (v / (1.0 + jnp.exp(-v))).astype(jnp.bfloat16)
+    half = 0.5 * v
+    return (half + half * jnp.tanh(half)).astype(jnp.bfloat16)
 
 
 def stack_taps(taps, own, edge):

time: 20 us -> 20 us (level)
  the two profiles are of different devices: /device:TPU:134 before, /device:TPU:70 now
where the time goes in v7:
time: 20 us; the launch traced here: 19.9 us
  Pallas kernels  19.1 us (96%)
  local copies, waits for them, and re-layouts  0.75 us (4%)
    pallas_call x1, Pallas kernels, on_device(): pl.pallas_call(functools.partial(kernel, tm, rows), out_shape=pltpu.VMEM(...  19.1 us
    unnamed x1, local copies, waits for them, and re-layouts  0.75 us

profile of v7, /device:TPU:70, one launch (start us, length us, event | category | flops | bytes accessed | tf_op | source)
XLA Modules:
  0.0 19.9 jit_solution(7052299468356944000)
XLA Ops:
  0.0 19.1 %residual_block.1 = bf16[4,96,2,256]{3,2,1,0:T(2,128)(2,1)S(1)} custom-call(bf16[4,96,2,256]{3,2,1,0:T(2,128)(2,1)} %feat_hbm.1, f32[96]{0:T(128)} %gain1_hbm.1, bf16[3,3,3,96,96]{4,3,2,1,0:T(8,128)(2,1)} %taps1_hbm.1, f32[96]{0:T(128)} %gain2_hbm.1, bf16[3,3,3,96,96]{4,3,2,1,0:T(8,128)(2,1)} %taps2_hbm.1), custom_call_target="tpu_custom_call" | custom-call | flops 2038431744 | bytes 3145728 | tf_op jit(solution)/shard_map/residual_block/pallas_call | solution.py:351
  19.1 0.7 %copy.7 = bf16[4,96,2,256]{3,2,1,0:T(2,128)(2,1)} copy(bf16[4,96,2,256]{3,2,1,0:T(2,128)(2,1)S(1)} %residual_block.1) | data formatting | bytes 786432
